TPU v7x, 32 devices: a whole 2x2x4 slice. The times are simulated.
32 devices in a mesh: dp: 4 (over z), lat: 2 (over x), lon: 4 (over y, core).
Axes of the slice: x: 2, y: 2, z: 4, core: 2. Of those that a mesh axis runs over, the one named last changes fastest.
Arguments:
- initial_state: float32 [4, 128, 16, 512], P('dp', None, 'lat', 'lon'), may hold values from -6 to 6
- cotangent: float32 [4, 128, 16, 512], P('dp', None, 'lat', 'lon'), may hold values from -6 to 6
- diffusion: float32 [128], replicated, may hold values from 0.02 to 0.2
- norm_gain: float32 [128], replicated, may hold values from 0.5 to 1.5
- weight_in: bfloat16 [1024, 128], replicated, may hold values from -0.5 to 0.5
- bias_in: float32 [1024], replicated, may hold values from -3 to 3
- weight_out: bfloat16 [128, 1024], replicated, may hold values from -0.1875 to 0.1875
Outputs:
- final_state: float32 [4, 128, 16, 512], P('dp', None, 'lat', 'lon')
- state_grad: float32 [4, 128, 16, 512], P('dp', None, 'lat', 'lon')
- grad_in: float32 [1024, 128], replicated
- grad_out: float32 [128, 1024], replicated
All inputs are finite; a program needn't handle non-finite values.
Results may differ from a plain program's by a relative error of at most 0.006.
Values sent between devices are 32-bit elements; how exact they have to be, the bound alone decides.
A program may use at most 64 MiB of HBM per device.

v0:
```python
import math

import jax
import jax.numpy as jnp
from jax import lax
from jax.sharding import PartitionSpec as P

ROLL = 2


EPSILON = 1e-05
CONTRACT_LAST = (((1,), (1,)), ((), ()))
CONTRACT_FIRST = (((0,), (0,)), ((), ()))


def with_halo(block, sides, width, periodic):
    for axis, dim in sides:
        count = lax.axis_size(axis)
        forward = [(i, i + 1) for i in range(count - 1)]
        if periodic:
            forward.append((count - 1, 0))
        backward = [(target, source) for source, target in forward]
        low = lax.ppermute(
            lax.slice_in_dim(block, block.shape[dim] - width, None, axis=dim), axis, forward
        )
        high = lax.ppermute(lax.slice_in_dim(block, 0, width, axis=dim), axis, backward)
        block = jnp.concatenate([low, block, high], axis=dim)
    return block


def laplace(field):
    rows_ext = with_halo(field, (("lat", 1),), 1, False)
    cols_ext = with_halo(field, (("lon", 2),), 1, True)
    return (
        rows_ext[:, 2:, :]
        + rows_ext[:, :-2, :]
        + cols_ext[:, :, 2:]
        + cols_ext[:, :, :-2]
        - 4.0 * field
    )


def diffuse(field, diffusion):
    return field + diffusion[:, None, None] * laplace(field)


def physics(mixed, norm_gain, weight_in, bias_in, weight_out):
    inverse = lax.rsqrt(jnp.mean(mixed * mixed, axis=0) + EPSILON)
    normed = (mixed * inverse * norm_gain[:, None, None]).astype(jnp.bfloat16)
    flat_normed = normed.reshape(normed.shape[0], -1)
    pre_act = jnp.dot(weight_in, flat_normed, preferred_element_type=jnp.float32) + bias_in[:, None]
    squashed = jnp.tanh(pre_act)
    hidden = squashed.astype(jnp.bfloat16)
    update = jnp.dot(weight_out, hidden, preferred_element_type=jnp.float32)
    return (mixed + update.reshape(mixed.shape), (inverse, flat_normed, squashed, hidden))


def on_device(initial_state, cotangent, diffusion, norm_gain, weight_in, bias_in, weight_out):
    field = initial_state[0]
    channels = field.shape[0]
    saved_fields = []
    saved_mixed = []
    for section in range(ROLL):
        mixed = diffuse(field, diffusion)
        saved_fields.append(field)
        saved_mixed.append(mixed)
        field, unused = physics(mixed, norm_gain, weight_in, bias_in, weight_out)
    adjoint = cotangent[0]
    sum_in = jnp.zeros(weight_in.shape, jnp.float32)
    sum_out = jnp.zeros(weight_out.shape, jnp.float32)
    for section in reversed(range(ROLL)):
        mixed = diffuse(saved_fields[section], diffusion)
        unused, cache = physics(mixed, norm_gain, weight_in, bias_in, weight_out)
        inverse, flat_normed, squashed, hidden = cache
        adjoint_flat = adjoint.reshape(channels, -1).astype(jnp.bfloat16)
        term_out = lax.dot_general(
            adjoint_flat, hidden, CONTRACT_LAST, preferred_element_type=jnp.float32
        )
        hidden_adj = lax.dot_general(
            weight_out, adjoint_flat, CONTRACT_FIRST, preferred_element_type=jnp.float32
        )
        pre_adj = (hidden_adj * (1.0 - squashed * squashed)).astype(jnp.bfloat16)
        term_in = lax.dot_general(
            pre_adj, flat_normed, CONTRACT_LAST, preferred_element_type=jnp.float32
        )
        sum_in = sum_in + term_in
        sum_out = sum_out + term_out
        normed_adj = lax.dot_general(
            weight_in, pre_adj, CONTRACT_FIRST, preferred_element_type=jnp.float32
        )
        scaled_adj = normed_adj.reshape(mixed.shape) * norm_gain[:, None, None]
        inner = jnp.sum(scaled_adj * mixed, axis=0)
        mixed_adj = adjoint + inverse * scaled_adj - mixed * inverse**3 * inner / channels
        adjoint = mixed_adj + diffusion[:, None, None] * laplace(mixed_adj)
    sum_in, sum_out = lax.psum((sum_in, sum_out), ("dp", "lat", "lon"))
    columns_all = (
        lax.axis_size("dp")
        * lax.axis_size("lat")
        * lax.axis_size("lon")
        * field.shape[1]
        * field.shape[2]
    )
    factor = jnp.float32(1.0 / math.sqrt(columns_all))
    return (field[None], adjoint[None], sum_in * factor, sum_out * factor)


def solution(mesh):
    in_specs = (P("dp", None, "lat", "lon"), P("dp", None, "lat", "lon"), P(), P(), P(), P(), P())
    out_specs = (P("dp", None, "lat", "lon"), P("dp", None, "lat", "lon"), P(), P())
    return jax.shard_map(
        on_device, mesh=mesh, in_specs=in_specs, out_specs=out_specs, check_vma=False
    )
```

profile of v0, /device:TPU:1, one launch (start us, length us, event | category | flops | bytes accessed | tf_op | source)
XLA Modules:
  0.0 244.2 jit_solution(16050792861114076286)
XLA Ops:
  9.9 4.0 %collective-permute-start.1 = (f32[128,1,128]{2,1,0:T(1,128)S(1)}, f32[128,1,128]{2,1,0:T(1,128)S(1)}, u32[]{:S(2)}, u32[]{:S(2)}) collective-permute-start(f32[128,1,128]{2,1,0:T(1,128)S(1)} %get-tuple-element.31), channel_id=1, source_target_pairs={{0,4},{1,5},{2,6},{3,7},{8,12},{9,13},{10,14},{11,15},{16,20},{17,... | collective-permute-start | bytes 196616 | tf_op jit(solution)/shard_map/ppermute | solution.py:23
  16.3 2.3 collective-permute-start.3
  18.6 12.4 %collective-permute-done.2 = f32[128,8,1]{2,1,0:T(8,128)S(1)} collective-permute-done((f32[128,8,1]{2,1,0:T(8,128)S(1)}, f32[128,8,1]{2,1,0:T(8,128)S(1)}, u32[]{:S(2)}, u32[]{:S(2)}) %collective-permute-start.2) | collective-permute-done | bytes 4128 | tf_op jit(solution)/shard_map/ppermute | solution.py:26
  31.0 2.6 %multiply_reduce_fusion.3 = (f32[8,128]{1,0:T(8,128)S(1)}, f32[128,8,128]{2,1,0:T(8,128)S(1)}) fusion(f32[128,8,128]{2,1,0:T(8,128)} %bitcast.68, f32[128,8,1]{2,1,0:T(8,128)S(1)} %collective-permute-done.3, f32[128,8,1]{2,1,0:T(8,128)S(1)} %collective-permute-done.2, f32[128,1,128]{2,1,0:T(1,128)S(1)} %collective-permute-done.1, ...), kind=kLoop, calls=%fused_computation.63 | loop fusion | flops 1702912 | bytes 1192448 | tf_op jit(solution)/shard_map/reduce_sum | solution.py:48
  35.4 2.0 copy-done.1
  39.8 4.0 %collective-permute-start.5 = (f32[128,1,128]{2,1,0:T(1,128)S(1)}, f32[128,1,128]{2,1,0:T(1,128)S(1)}, u32[]{:S(2)}, u32[]{:S(2)}) collective-permute-start(f32[128,1,128]{2,1,0:T(1,128)S(1)} %get-tuple-element.27), channel_id=1, source_target_pairs={{0,4},{1,5},{2,6},{3,7},{8,12},{9,13},{10,14},{11,15},{16,20},{17,... | collective-permute-start | bytes 196616 | tf_op jit(solution)/shard_map/ppermute | solution.py:23
  46.6 11.4 %collective-permute-done.6 = f32[128,8,1]{2,1,0:T(8,128)S(1)} collective-permute-done((f32[128,8,1]{2,1,0:T(8,128)S(1)}, f32[128,8,1]{2,1,0:T(8,128)S(1)}, u32[]{:S(2)}, u32[]{:S(2)}) %collective-permute-start.6) | collective-permute-done | bytes 4128 | tf_op jit(solution)/shard_map/ppermute | solution.py:26
  60.3 2.0 copy-done.3
  64.1 3.2 %fusion = bf16[1024,1024]{0,1:T(8,128)(2,1)S(1)} fusion(f32[1024,1024]{1,0:T(8,128)} %copy-done.3, bf16[128,1024]{1,0:T(8,128)(2,1)S(1)} %copy-done, f32[1024]{0:T(1024)S(1)} %copy-done.13, bf16[16,8,8,128]{3,2,1,0:T(8,128)(2,1)} %bitcast.69), kind=kOutput, calls=%fused_computation.1 | convolution fusion | flops 273678336 | bytes 6819840 | tf_op jit(solution)/shard_map/dot_general | solution.py:79
  67.3 2.5 %fusion.68 = f32[1024,128]{1,0:T(8,128)} fusion(bf16[1024,1024]{0,1:T(8,128)(2,1)S(1)} %fusion, bf16[1024,128]{1,0:T(8,128)(2,1)} %param.11), kind=kOutput, calls=%fused_computation.98 | convolution fusion | flops 268435456 | bytes 2883584 | tf_op jit(solution)/shard_map/dot_general | solution.py:88
  69.8 2.0 copy.14
  73.1 2.3 fusion.36
  75.7 1.6 collective-permute-start.8
  77.3 4.0 %collective-permute-start.9 = (f32[128,1,128]{2,1,0:T(1,128)S(1)}, f32[128,1,128]{2,1,0:T(1,128)S(1)}, u32[]{:S(2)}, u32[]{:S(2)}) collective-permute-start(f32[128,1,128]{2,1,0:T(1,128)S(1)} %get-tuple-element.21), channel_id=1, source_target_pairs={{0,4},{1,5},{2,6},{3,7},{8,12},{9,13},{10,14},{11,15},{16,20},{17,... | collective-permute-start | bytes 196616 | tf_op jit(solution)/shard_map/ppermute | solution.py:23
  81.3 1.6 collective-permute-start.10
  84.6 11.3 %collective-permute-done.10 = f32[128,8,1]{2,1,0:T(8,128)S(1)} collective-permute-done((f32[128,8,1]{2,1,0:T(8,128)S(1)}, f32[128,8,1]{2,1,0:T(8,128)S(1)}, u32[]{:S(2)}, u32[]{:S(2)}) %collective-permute-start.10) | collective-permute-done | bytes 4128 | tf_op jit(solution)/shard_map/ppermute | solution.py:26
  99.7 1.6 fusion.3
  102.1 1.5 convolution_add_fusion
  105.7 4.0 %collective-permute-start.13 = (f32[128,1,128]{2,1,0:T(1,128)S(1)}, f32[128,1,128]{2,1,0:T(1,128)S(1)}, u32[]{:S(2)}, u32[]{:S(2)}) collective-permute-start(f32[128,1,128]{2,1,0:T(1,128)S(1)} %get-tuple-element.17), channel_id=1, source_target_pairs={{0,4},{1,5},{2,6},{3,7},{8,12},{9,13},{10,14},{11,15},{16,20},{17,... | collective-permute-start | bytes 196616 | tf_op jit(solution)/shard_map/ppermute | solution.py:23
  109.9 1.5 collective-permute-start.14
  112.0 13.6 %collective-permute-done.14 = f32[128,8,1]{2,1,0:T(8,128)S(1)} collective-permute-done((f32[128,8,1]{2,1,0:T(8,128)S(1)}, f32[128,8,1]{2,1,0:T(8,128)S(1)}, u32[]{:S(2)}, u32[]{:S(2)}) %collective-permute-start.14) | collective-permute-done | bytes 4128 | tf_op jit(solution)/shard_map/ppermute | solution.py:26
  125.5 1.4 fusion.15
  126.9 106.5 %all-reduce.3.cloned.1.call-done = (f32[1024,128]{1,0:T(8,128)}, f32[128,1024]{0,1:T(8,128)}) async-done(((f32[1024,128]{1,0:T(8,128)}, f32[128,1024]{0,1:T(8,128)}), (f32[1024,128]{1,0:T(8,128)}, f32[128,1024]{0,1:T(8,128)})) %all-reduce.3.cloned.1.call-update) | async-done | bytes 1048592 | tf_op jit(solution)/shard_map/psum | solution.py:95
  233.4 1.9 broadcast_multiply_fusion.1
  (84 shorter events, 28.7 us)
Async XLA Ops:
  7.2 30.2 %copy-start = (bf16[128,1024]{1,0:T(8,128)(2,1)S(1)}, bf16[128,1024]{1,0:T(8,128)(2,1)}, u32[]{:S(2)}) copy-start(bf16[128,1024]{1,0:T(8,128)(2,1)} %param.13) | copy-start | bytes 786436
  7.2 26.5 %copy-start.14 = (f32[128]{0:T(128)S(1)}, f32[128]{0:T(128)}, u32[]{:S(2)}) copy-start(f32[128]{0:T(128)} %param.10) | copy-start | bytes 1540
  7.2 27.4 %copy-start.5 = (bf16[1024,128]{1,0:T(8,128)(2,1)S(1)}, bf16[1024,128]{1,0:T(8,128)(2,1)}, u32[]{:S(2)}) copy-start(bf16[1024,128]{1,0:T(8,128)(2,1)} %param.11) | copy-start | bytes 786436
  7.2 226.2 %all-reduce.3.cloned.1.call-start = ((), (), s32[]{:S(2)}) async-start(), calls=%async_computation | async-start | bytes 2097152 | tf_op jit(solution)/shard_map/psum | solution.py:95
  8.6 22.4 %collective-permute-start = (f32[128,1,128]{2,1,0:T(1,128)S(1)}, f32[128,1,128]{2,1,0:T(1,128)S(1)}, u32[]{:S(2)}, u32[]{:S(2)}) collective-permute-start(f32[128,1,128]{2,1,0:T(1,128)S(1)} %get-tuple-element.30), channel_id=1, source_target_pairs={{4,0},{5,1},{6,2},{7,3},{12,8},{13,9},{14,10},{15,11},{20,16},{21,... | collective-permute-start | bytes 196616 | tf_op jit(solution)/shard_map/ppermute | solution.py:26
  9.9 21.1 %collective-permute-start.1 = (f32[128,1,128]{2,1,0:T(1,128)S(1)}, f32[128,1,128]{2,1,0:T(1,128)S(1)}, u32[]{:S(2)}, u32[]{:S(2)}) collective-permute-start(f32[128,1,128]{2,1,0:T(1,128)S(1)} %get-tuple-element.31), channel_id=1, source_target_pairs={{0,4},{1,5},{2,6},{3,7},{8,12},{9,13},{10,14},{11,15},{16,20},{17,... | collective-permute-start | bytes 196616 | tf_op jit(solution)/shard_map/ppermute | solution.py:23
  15.3 22.0 %copy-start.13 = (f32[1024]{0:T(1024)S(1)}, f32[1024]{0:T(1024)}, u32[]{:S(2)}) copy-start(f32[1024]{0:T(1024)} %param.12) | copy-start | bytes 12292
  15.3 15.7 %collective-permute-start.2 = (f32[128,8,1]{2,1,0:T(8,128)S(1)}, f32[128,8,1]{2,1,0:T(8,128)S(1)}, u32[]{:S(2)}, u32[]{:S(2)}) collective-permute-start(f32[128,8,1]{2,1,0:T(8,128)S(1)} %get-tuple-element.32), channel_id=1, source_target_pairs={{1,0},{2,1},{3,2},{0,3},{5,4},{6,5},{7,6},{4,7},{9,8},{10,9},{11,1... | collective-permute-start | bytes 12296 | tf_op jit(solution)/shard_map/ppermute | solution.py:26
  16.3 14.7 %collective-permute-start.3 = (f32[128,8,1]{2,1,0:T(8,128)S(1)}, f32[128,8,1]{2,1,0:T(8,128)S(1)}, u32[]{:S(2)}, u32[]{:S(2)}) collective-permute-start(f32[128,8,1]{2,1,0:T(8,128)S(1)} %get-tuple-element.33), channel_id=1, source_target_pairs={{0,1},{1,2},{2,3},{3,0},{4,5},{5,6},{6,7},{7,4},{8,9},{9,10},{10,1... | collective-permute-start | bytes 12296 | tf_op jit(solution)/shard_map/ppermute | solution.py:23
  37.3 20.7 %copy-start.15 = (f32[128]{0:T(128)S(1)}, f32[128]{0:T(128)}, u32[]{:S(2)}) copy-start(f32[128]{0:T(128)} %param.9) | copy-start | bytes 1540
  38.5 19.5 %collective-permute-start.4 = (f32[128,1,128]{2,1,0:T(1,128)S(1)}, f32[128,1,128]{2,1,0:T(1,128)S(1)}, u32[]{:S(2)}, u32[]{:S(2)}) collective-permute-start(f32[128,1,128]{2,1,0:T(1,128)S(1)} %get-tuple-element.26), channel_id=1, source_target_pairs={{4,0},{5,1},{6,2},{7,3},{12,8},{13,9},{14,10},{15,11},{20,16},{21,... | collective-permute-start | bytes 196616 | tf_op jit(solution)/shard_map/ppermute | solution.py:26
  39.8 18.2 %collective-permute-start.5 = (f32[128,1,128]{2,1,0:T(1,128)S(1)}, f32[128,1,128]{2,1,0:T(1,128)S(1)}, u32[]{:S(2)}, u32[]{:S(2)}) collective-permute-start(f32[128,1,128]{2,1,0:T(1,128)S(1)} %get-tuple-element.27), channel_id=1, source_target_pairs={{0,4},{1,5},{2,6},{3,7},{8,12},{9,13},{10,14},{11,15},{16,20},{17,... | collective-permute-start | bytes 196616 | tf_op jit(solution)/shard_map/ppermute | solution.py:23
  44.0 14.0 %collective-permute-start.6 = (f32[128,8,1]{2,1,0:T(8,128)S(1)}, f32[128,8,1]{2,1,0:T(8,128)S(1)}, u32[]{:S(2)}, u32[]{:S(2)}) collective-permute-start(f32[128,8,1]{2,1,0:T(8,128)S(1)} %get-tuple-element.28), channel_id=1, source_target_pairs={{1,0},{2,1},{3,2},{0,3},{5,4},{6,5},{7,6},{4,7},{9,8},{10,9},{11,1... | collective-permute-start | bytes 12296 | tf_op jit(solution)/shard_map/ppermute | solution.py:26
  45.3 12.7 %collective-permute-start.7 = (f32[128,8,1]{2,1,0:T(8,128)S(1)}, f32[128,8,1]{2,1,0:T(8,128)S(1)}, u32[]{:S(2)}, u32[]{:S(2)}) collective-permute-start(f32[128,8,1]{2,1,0:T(8,128)S(1)} %get-tuple-element.29), channel_id=1, source_target_pairs={{0,1},{1,2},{2,3},{3,0},{4,5},{5,6},{6,7},{7,4},{8,9},{9,10},{10,1... | collective-permute-start | bytes 12296 | tf_op jit(solution)/shard_map/ppermute | solution.py:23
  71.8 12.0 %copy-start.11 = (bf16[128,8,128]{2,1,0:T(8,128)(2,1)S(1)}, bf16[128,8,128]{2,1,0:T(8,128)(2,1)}, u32[]{:S(2)}) copy-start(bf16[128,8,128]{2,1,0:T(8,128)(2,1)} %copy-done.10) | copy-start | bytes 786436
  75.7 20.8 %copy-start.2 = (f32[1024,1024]{1,0:T(8,128)S(1)}, f32[1024,1024]{1,0:T(8,128)}, u32[]{:S(2)}) copy-start(f32[1024,1024]{1,0:T(8,128)} %copy-done.1) | copy-start | bytes 12582916
  75.7 20.1 %collective-permute-start.8 = (f32[128,1,128]{2,1,0:T(1,128)S(1)}, f32[128,1,128]{2,1,0:T(1,128)S(1)}, u32[]{:S(2)}, u32[]{:S(2)}) collective-permute-start(f32[128,1,128]{2,1,0:T(1,128)S(1)} %get-tuple-element.20), channel_id=1, source_target_pairs={{4,0},{5,1},{6,2},{7,3},{12,8},{13,9},{14,10},{15,11},{20,16},{21,... | collective-permute-start | bytes 196616 | tf_op jit(solution)/shard_map/ppermute | solution.py:26
  77.3 18.6 %collective-permute-start.9 = (f32[128,1,128]{2,1,0:T(1,128)S(1)}, f32[128,1,128]{2,1,0:T(1,128)S(1)}, u32[]{:S(2)}, u32[]{:S(2)}) collective-permute-start(f32[128,1,128]{2,1,0:T(1,128)S(1)} %get-tuple-element.21), channel_id=1, source_target_pairs={{0,4},{1,5},{2,6},{3,7},{8,12},{9,13},{10,14},{11,15},{16,20},{17,... | collective-permute-start | bytes 196616 | tf_op jit(solution)/shard_map/ppermute | solution.py:23
  81.3 14.6 %collective-permute-start.10 = (f32[128,8,1]{2,1,0:T(8,128)S(1)}, f32[128,8,1]{2,1,0:T(8,128)S(1)}, u32[]{:S(2)}, u32[]{:S(2)}) collective-permute-start(f32[128,8,1]{2,1,0:T(8,128)S(1)} %get-tuple-element.22), channel_id=1, source_target_pairs={{1,0},{2,1},{3,2},{0,3},{5,4},{6,5},{7,6},{4,7},{9,8},{10,9},{11,1... | collective-permute-start | bytes 12296 | tf_op jit(solution)/shard_map/ppermute | solution.py:26
  82.8 13.0 %collective-permute-start.11 = (f32[128,8,1]{2,1,0:T(8,128)S(1)}, f32[128,8,1]{2,1,0:T(8,128)S(1)}, u32[]{:S(2)}, u32[]{:S(2)}) collective-permute-start(f32[128,8,1]{2,1,0:T(8,128)S(1)} %get-tuple-element.23), channel_id=1, source_target_pairs={{0,1},{1,2},{2,3},{3,0},{4,5},{5,6},{6,7},{7,4},{8,9},{9,10},{10,1... | collective-permute-start | bytes 12296 | tf_op jit(solution)/shard_map/ppermute | solution.py:23
  104.4 21.1 %collective-permute-start.12 = (f32[128,1,128]{2,1,0:T(1,128)S(1)}, f32[128,1,128]{2,1,0:T(1,128)S(1)}, u32[]{:S(2)}, u32[]{:S(2)}) collective-permute-start(f32[128,1,128]{2,1,0:T(1,128)S(1)} %get-tuple-element.16), channel_id=1, source_target_pairs={{4,0},{5,1},{6,2},{7,3},{12,8},{13,9},{14,10},{15,11},{20,16},{21,... | collective-permute-start | bytes 196616 | tf_op jit(solution)/shard_map/ppermute | solution.py:26
  105.7 19.8 %collective-permute-start.13 = (f32[128,1,128]{2,1,0:T(1,128)S(1)}, f32[128,1,128]{2,1,0:T(1,128)S(1)}, u32[]{:S(2)}, u32[]{:S(2)}) collective-permute-start(f32[128,1,128]{2,1,0:T(1,128)S(1)} %get-tuple-element.17), channel_id=1, source_target_pairs={{0,4},{1,5},{2,6},{3,7},{8,12},{9,13},{10,14},{11,15},{16,20},{17,... | collective-permute-start | bytes 196616 | tf_op jit(solution)/shard_map/ppermute | solution.py:23
  109.9 15.6 %collective-permute-start.14 = (f32[128,8,1]{2,1,0:T(8,128)S(1)}, f32[128,8,1]{2,1,0:T(8,128)S(1)}, u32[]{:S(2)}, u32[]{:S(2)}) collective-permute-start(f32[128,8,1]{2,1,0:T(8,128)S(1)} %get-tuple-element.18), channel_id=1, source_target_pairs={{1,0},{2,1},{3,2},{0,3},{5,4},{6,5},{7,6},{4,7},{9,8},{10,9},{11,1... | collective-permute-start | bytes 12296 | tf_op jit(solution)/shard_map/ppermute | solution.py:26
  111.4 14.1 %collective-permute-start.15 = (f32[128,8,1]{2,1,0:T(8,128)S(1)}, f32[128,8,1]{2,1,0:T(8,128)S(1)}, u32[]{:S(2)}, u32[]{:S(2)}) collective-permute-start(f32[128,8,1]{2,1,0:T(8,128)S(1)} %get-tuple-element.19), channel_id=1, source_target_pairs={{0,1},{1,2},{2,3},{3,0},{4,5},{5,6},{6,7},{7,4},{8,9},{9,10},{10,1... | collective-permute-start | bytes 12296 | tf_op jit(solution)/shard_map/ppermute | solution.py:23
  (9 other events, 22.3 us)
Sparse Core Ops, SparseCore 0:
  104.2 129.1 all-reduce.2
where the time goes:
time: 246 us; the launch traced here: 244 us
  waiting for transfers between devices  155 us (63%)
  starting transfers between devices  31.2 us (13%)
  matrix products  15.2 us (6%)
  local copies, waits for them, and re-layouts  14.8 us (6%)
  between operations  14.4 us (6%)
  other arithmetic  13.5 us (5%)
    psum x1, waiting for transfers between devices, on_device(): sum_in, sum_out = lax.psum((sum_in, sum_out), ('dp', 'lat', 'lon'))  106 us
    ppermute x8, waiting for transfers between devices, with_halo(): lax.ppermute(lax.slice_in_dim(block, 0, width, axis=dim), axis, backward)  48.6 us
    ppermute x8, starting transfers between devices, with_halo(): lax.ppermute(lax.slice_in_dim(block, block.shape[dim] - width, None, axis...  20.4 us
    ppermute x8, starting transfers between devices, with_halo(): lax.ppermute(lax.slice_in_dim(block, 0, width, axis=dim), axis, backward)  10.8 us
    unnamed x33, local copies, waits for them, and re-layouts  7.65 us
  transfers between devices with their start and end apart: 17, of which 5 were waited for; matrix products, arithmetic and copies ran while one was open for 2% of the time, Pallas kernels for 0%

commit v1 on v0

v1 whole, which is shorter than its diff:
```python
import functools
import math

import jax
import jax.numpy as jnp
from jax import lax
from jax.experimental import pallas as pl
from jax.experimental.pallas import tpu as pltpu
from jax.sharding import PartitionSpec as P

EPSILON = 1e-05
MESH = pl.DeviceIdType.MESH
F32 = jnp.float32
BF16 = jnp.bfloat16
NT = (((1,), (1,)), ((), ()))


def make_plan(sizes, hidden):
    pair = 2 if sizes["lon"] % 2 == 0 else 1
    counts = {"core": pair, "high": sizes["lon"] // pair, "lat": sizes["lat"], "dp": sizes["dp"]}
    orders = (("core", "high", "lat", "dp"), ("core", "lat", "high", "dp"))
    plan, slot, sem = [], 0, 0
    for stream in range(2):
        for part, order in enumerate(orders):
            rows = hidden // len(orders)
            start = stream * hidden + part * rows
            phases = []
            length = rows
            for axis in order:
                n = counts[axis]
                if n == 1:
                    continue
                if length % (8 * n) == 0:
                    shard = length // n
                    phases.append(("scatter", axis, n, shard, slot, sem, sem + n - 1))
                    slot += (n - 1) * shard
                    sem += 2 * (n - 1)
                    length = shard
                else:
                    phases.append(("reduce", axis, n, length, slot, sem, None))
                    slot += n * length
                    sem += n - 1
            plan.append((start, rows, phases))
    return pair, plan, max(slot, 8), max(sem, 1)


def kernel(
    sizes, factor,
    x_hbm, cot_hbm, dif, gain, win_hbm, bias, wout_hbm,
    fin_hbm, sg_hbm, gin_hbm, gout_hbm,
    xin, cot, win, wout, winT, woutT, biasb,
    F0, F1, M0, M1, ADJ, MA, ADJB, NB0, NB1, INV, HID0, HID1, D0, HA, PA,
    acc, res, slots, packed, halo_lat, halo_lon, fin_v, sg_v,
    load_sem, store_sem, lat_send, lat_recv, lon_send, lon_recv, red_send, red_recv,
):
    C, R, L = xin.shape
    H = win.shape[0]
    n_lat, n_lon, n_dp = sizes["lat"], sizes["lon"], sizes["dp"]
    lat, lon, dp = lax.axis_index("lat"), lax.axis_index("lon"), lax.axis_index("dp")
    pair, plan, _, _ = make_plan(sizes, H)
    n_high = n_lon // pair
    core, high = lax.rem(lon, pair), lon // pair

    loads = [
        pltpu.make_async_copy(x_hbm.at[0], xin, load_sem.at[0]),
        pltpu.make_async_copy(win_hbm, win, load_sem.at[1]),
        pltpu.make_async_copy(wout_hbm, wout, load_sem.at[2]),
        pltpu.make_async_copy(cot_hbm.at[0], cot, load_sem.at[3]),
    ]
    for copy in loads:
        copy.start()

    barrier = pltpu.get_barrier_semaphore()
    total = 0
    for name, n, i in (("lon", n_lon, lon), ("lat", n_lat, lat), ("dp", n_dp, dp)):
        for k in range(1, n):
            pl.semaphore_signal(barrier, inc=1, device_id={name: lax.rem(i + k, n)}, device_id_type=MESH)
            total += 1

    lane = lax.broadcasted_iota(jnp.int32, (C, L), 1)

    def pack(e, src):
        out = jnp.zeros((C, L), F32)
        for r in range(R):
            row = src[r]
            first = pltpu.roll(row, r, 1) if r else row
            last = pltpu.roll(row, R + r + 1, 1)
            out = jnp.where(lane == r, first, jnp.where(lane == R + r, last, out))
        packed[e] = out.T[: 2 * R, :]

    def lat_copies(e, src):
        down = functools.partial(
            pltpu.make_async_remote_copy,
            src_ref=src.at[R - 1], dst_ref=halo_lat.at[e, 0],
            send_sem=lat_send.at[e, 0], recv_sem=lat_recv.at[e, 0],
            device_id={"lat": lax.rem(lat + 1, n_lat)}, device_id_type=MESH)
        up = functools.partial(
            pltpu.make_async_remote_copy,
            src_ref=src.at[0], dst_ref=halo_lat.at[e, 1],
            send_sem=lat_send.at[e, 1], recv_sem=lat_recv.at[e, 1],
            device_id={"lat": lax.rem(lat + n_lat - 1, n_lat)}, device_id_type=MESH)
        return down, up

    def lon_copies(e):
        right = pltpu.make_async_remote_copy(
            src_ref=packed.at[e, pl.ds(R, R)], dst_ref=halo_lon.at[e, pl.ds(0, R)],
            send_sem=lon_send.at[e, 0], recv_sem=lon_recv.at[e, 0],
            device_id={"lon": lax.rem(lon + 1, n_lon)}, device_id_type=MESH)
        left = pltpu.make_async_remote_copy(
            src_ref=packed.at[e, pl.ds(0, R)], dst_ref=halo_lon.at[e, pl.ds(R, R)],
            send_sem=lon_send.at[e, 1], recv_sem=lon_recv.at[e, 1],
            device_id={"lon": lax.rem(lon + n_lon - 1, n_lon)}, device_id_type=MESH)
        return right, left

    def send_lat(e, src):
        down, up = lat_copies(e, src)

        @pl.when(lat < n_lat - 1)
        def _():
            down().start()

        @pl.when(lat > 0)
        def _():
            up().start()

    def send_lon(e, src):
        pack(e, src)
        for copy in lon_copies(e):
            copy.start()

    def wait_halo(e, src):
        down, up = lat_copies(e, src)

        @pl.when(lat > 0)
        def _():
            down().wait_recv()

        @pl.when(lat == 0)
        def _():
            halo_lat[e, 0] = jnp.zeros((C, L), F32)

        @pl.when(lat < n_lat - 1)
        def _():
            up().wait_recv()

        @pl.when(lat == n_lat - 1)
        def _():
            halo_lat[e, 1] = jnp.zeros((C, L), F32)

        for copy in lon_copies(e):
            copy.wait_recv()

    def wait_sent(e, src):
        down, up = lat_copies(e, src)

        @pl.when(lat < n_lat - 1)
        def _():
            down().wait_send()

        @pl.when(lat > 0)
        def _():
            up().wait_send()

        for copy in lon_copies(e):
            copy.wait_send()

    def diffuse(e, src, put):
        side = halo_lon[e].T
        dT = jnp.broadcast_to(dif[...], (L, C)).T
        for r in range(R):
            here = src[r]
            above = src[r - 1] if r else halo_lat[e, 0]
            below = src[r + 1] if r < R - 1 else halo_lat[e, 1]
            west = jnp.where(lane == 0, pltpu.roll(side, L - r, 1) if r else side, pltpu.roll(here, 1, 1))
            east = jnp.where(lane == L - 1, pltpu.roll(side, L - 1 - R - r, 1), pltpu.roll(here, L - 1, 1))
            put(r, here + dT * (below + above + east + west - 4.0 * here))

    def normalise(t, r, m, nb, gT):
        inv = lax.rsqrt(jnp.sum(m * m, axis=0, keepdims=True) * (1.0 / C) + EPSILON)
        INV[t, r] = inv
        nb[:, r * L:(r + 1) * L] = (m * inv * gT).astype(BF16)

    W = 2 * L
    HB = 256

    def span(q, width):
        return pl.ds(pl.multiple_of(q * width, width), width)

    def line(axis, i_n):
        if axis == "core":
            return core, lambda p: {"lon": high * pair + p}
        if axis == "high":
            return high, lambda p: {"lon": p * pair + core}
        if axis == "lat":
            return lat, lambda p: {"lat": p}
        return dp, lambda p: {"dp": p}

    sent = []

    def substream(start, rows, phases):
        base, length = start, rows
        done = []
        for kind, axis, n, size, slot, sem, gsem in phases:
            i, device = line(axis, n)
            copies = []
            for k in range(1, n):
                p = lax.rem(i + k, n)
                if kind == "scatter":
                    src = acc.at[pl.ds(pl.multiple_of(base + p * size, 8), size)]
                    dst = slots.at[pl.ds(slot + (k - 1) * size, size)]
                else:
                    src = acc.at[pl.ds(pl.multiple_of(base, 8), size)]
                    dst = slots.at[pl.ds(pl.multiple_of(slot + i * size, 8), size)]
                copy = pltpu.make_async_remote_copy(
                    src_ref=src, dst_ref=dst, send_sem=red_send.at[sem + k - 1], recv_sem=red_recv.at[sem + k - 1],
                    device_id=device(p), device_id_type=MESH)
                copy.start()
                copies.append(copy)
            if kind == "scatter":
                sent.extend(copies)
                done.append((base, axis, n, size, gsem))
                base, length = base + i * size, size
            mine = pl.ds(pl.multiple_of(base, 8), length)
            if kind == "reduce":
                slots[pl.ds(pl.multiple_of(slot + i * size, 8), size)] = acc[mine]
            yield
            for copy in copies:
                copy.wait_recv()
            if kind == "scatter":
                value = acc[mine]
                for k in range(n - 1):
                    value = value + slots[pl.ds(slot + k * size, size)]
            else:
                for copy in copies:
                    copy.wait_send()
                value = slots[pl.ds(slot, size)]
                for k in range(1, n):
                    value = value + slots[pl.ds(slot + k * size, size)]
            acc[mine] = value
        mine = pl.ds(pl.multiple_of(base, 8), length)
        res[mine] = acc[mine] * factor
        for parent, axis, n, size, gsem in reversed(done):
            i, device = line(axis, n)
            here = pl.ds(pl.multiple_of(parent + i * size, 8), size)
            copies = []
            for k in range(1, n):
                copy = pltpu.make_async_remote_copy(
                    src_ref=res.at[here], dst_ref=res.at[here],
                    send_sem=red_send.at[gsem + k - 1], recv_sem=red_recv.at[gsem + k - 1],
                    device_id=device(lax.rem(i + k, n)), device_id_type=MESH)
                copy.start()
                copies.append(copy)
            sent.extend(copies)
            yield
            for copy in copies:
                copy.wait_recv()

    streams = [substream(*p) for p in plan]
    n_in = len(plan) // 2
    in_streams, out_streams = streams[:n_in], streams[n_in:]

    def advance(group):
        going = False
        for g in group:
            going = next(g, "end") is None or going
        return going

    loads[0].wait()
    for r in range(R):
        F0[r] = xin[:, r, :]
    for e in range(4):
        halo_lon[e, 2 * R:, :] = jnp.zeros((L - 2 * R, C), F32)
    if total:
        pl.semaphore_wait(barrier, total)
    send_lat(0, F0)
    send_lon(0, F0)
    gT = jnp.broadcast_to(gain[...], (L, C)).T
    for b in range(H // L):
        biasb[b * L:(b + 1) * L, :] = jnp.broadcast_to(bias[b:b + 1, :], (L, L)).T
    loads[1].wait()
    loads[2].wait()
    winT[...] = win[...].T
    woutT[...] = wout[...].T
    loads[3].wait()
    for r in range(R):
        a = cot[:, r, :]
        ADJ[r] = a
        ADJB[:, r * L:(r + 1) * L] = a.astype(BF16)
    wait_halo(0, F0)

    def put_m0(r, m):
        M0[r] = m
        normalise(0, r, m, NB0, gT)

    diffuse(0, F0, put_m0)

    def forward0(q, carry):
        cols = span(q, W)
        nq = NB0[:, cols]
        update = jnp.zeros((C, W), F32)
        for h in range(0, H, HB):
            b = biasb[h:h + HB, :]
            s = jnp.tanh(jnp.dot(win[h:h + HB, :], nq, preferred_element_type=F32) + jnp.concatenate([b, b], 1))
            D0[h:h + HB, cols] = 1.0 - s * s
            hid = s.astype(BF16)
            HID0[h:h + HB, cols] = hid
            update = update + jnp.dot(wout[:, h:h + HB], hid, preferred_element_type=F32)
        F1[2 * q] = M0[2 * q] + update[:, :L]
        F1[2 * q + 1] = M0[2 * q + 1] + update[:, L:]
        return carry

    lax.fori_loop(0, R // 2, forward0, 0)
    send_lat(1, F1)
    send_lon(1, F1)

    def early_adjoint(q, carry):
        cols = span(q, W)
        aq = ADJB[:, cols]
        for h in range(0, H, HB):
            HA[h:h + HB, cols] = jnp.dot(woutT[h:h + HB, :], aq, preferred_element_type=F32)
        return carry

    lax.fori_loop(0, R // 2, early_adjoint, 0)
    wait_halo(1, F1)

    def put_m1(r, m):
        M1[r] = m
        normalise(1, r, m, NB1, gT)

    diffuse(1, F1, put_m1)

    def mix(t, r, M, na, gt):
        m = M[r]
        inv = INV[t, r]
        scaled = gt * na
        inner = jnp.sum(scaled * m, axis=0, keepdims=True)
        MA[r] = ADJ[r] + inv * scaled - m * (inv * inv * inv * inner * (1.0 / C))

    def forward1(q, carry):
        cols = span(q, W)
        nq = NB1[:, cols]
        update = jnp.zeros((C, W), F32)
        na = jnp.zeros((C, W), F32)
        for h in range(0, H, HB):
            b = biasb[h:h + HB, :]
            s = jnp.tanh(jnp.dot(win[h:h + HB, :], nq, preferred_element_type=F32) + jnp.concatenate([b, b], 1))
            pa = (HA[h:h + HB, cols] * (1.0 - s * s)).astype(BF16)
            PA[h:h + HB, cols] = pa
            na = na + jnp.dot(winT[:, h:h + HB], pa, preferred_element_type=F32)
            hid = s.astype(BF16)
            HID1[h:h + HB, cols] = hid
            update = update + jnp.dot(wout[:, h:h + HB], hid, preferred_element_type=F32)
        gt = jnp.broadcast_to(gain[...], (L, C)).T
        for k in range(2):
            F0[2 * q + k] = M1[2 * q + k] + update[:, k * L:(k + 1) * L]
            mix(1, 2 * q + k, M1, na[:, k * L:(k + 1) * L], gt)
        return carry

    wait_sent(0, F0)
    lax.fori_loop(0, R // 2, forward1, 0)
    send_lat(2, MA)
    send_lon(2, MA)

    def terms_out(hid_ref, add):
        def body(j, carry):
            rows = span(j, HB)
            t = lax.dot_general(ADJB[...], hid_ref[rows, :], NT, preferred_element_type=F32)
            for k in range(HB // L):
                at = pl.ds(pl.multiple_of(H + j * HB + k * L, L), C)
                part = t[:, k * L:(k + 1) * L]
                acc[at, :] = acc[at, :] + part if add else part
            return carry
        lax.fori_loop(0, H // HB, body, 0)

    def terms_in(nb, add, lo, hi):
        def body(j, carry):
            rows = span(j, HB)
            t = lax.dot_general(PA[rows, :], nb[...], NT, preferred_element_type=F32)
            acc[rows, :] = acc[rows, :] + t if add else t
            return carry
        lax.fori_loop(lo, hi, body, 0)

    terms_out(HID1, False)
    terms_in(NB1, False, 0, H // HB)
    for r in range(R):
        fin_v[:, r, :] = F0[r]
    fin_store = pltpu.make_async_copy(fin_v, fin_hbm.at[0], store_sem.at[0])
    fin_store.start()
    wait_halo(2, MA)

    def put_adj(r, a):
        ADJ[r] = a
        ADJB[:, r * L:(r + 1) * L] = a.astype(BF16)

    diffuse(2, MA, put_adj)
    terms_out(HID0, True)
    advance(out_streams)

    def back0(q, carry):
        cols = span(q, W)
        aq = ADJB[:, cols]
        for h in range(0, H, HB):
            ha = jnp.dot(woutT[h:h + HB, :], aq, preferred_element_type=F32)
            PA[h:h + HB, cols] = (ha * D0[h:h + HB, cols]).astype(BF16)
        return carry

    lax.fori_loop(0, R // 2, back0, 0)
    advance(out_streams)
    blocks = H // HB
    for s, g in enumerate(in_streams):
        terms_in(NB0, True, s * blocks // n_in, (s + 1) * blocks // n_in)
        next(g, None)
    wait_sent(2, MA)

    def back1(q, carry):
        cols = span(q, W)
        na = jnp.dot(winT[...], PA[:, cols], preferred_element_type=F32)
        gt = jnp.broadcast_to(gain[...], (L, C)).T
        for k in range(2):
            mix(0, 2 * q + k, M0, na[:, k * L:(k + 1) * L], gt)
        return carry

    lax.fori_loop(0, R // 2, back1, 0)
    send_lat(3, MA)
    send_lon(3, MA)
    advance(out_streams)
    advance(in_streams)
    wait_halo(3, MA)

    def put_grad(r, a):
        sg_v[:, r, :] = a

    diffuse(3, MA, put_grad)
    sg_store = pltpu.make_async_copy(sg_v, sg_hbm.at[0], store_sem.at[1])
    sg_store.start()
    stores = [fin_store, sg_store]
    out_going = in_going = True
    while out_going or in_going:
        if out_going:
            out_going = advance(out_streams)
            if not out_going:
                for b in range(H // L):
                    copy = pltpu.make_async_copy(
                        res.at[pl.ds(H + b * L, C)], gout_hbm.at[:, pl.ds(b * L, L)], store_sem.at[3 + b])
                    copy.start()
                    stores.append(copy)
        if in_going:
            in_going = advance(in_streams)
            if not in_going:
                copy = pltpu.make_async_copy(res.at[pl.ds(0, H)], gin_hbm, store_sem.at[2])
                copy.start()
                stores.append(copy)
    for copy in sent:
        copy.wait_send()
    wait_sent(1, F1)
    wait_sent(3, MA)
    for copy in stores:
        copy.wait()


def solution(mesh):
    sizes = {name: mesh.shape[name] for name in ("dp", "lat", "lon")}
    state = P("dp", None, "lat", "lon")

    def on_device(initial_state, cotangent, diffusion, norm_gain, weight_in, bias_in, weight_out):
        _, C, R, L = initial_state.shape
        H = weight_in.shape[0]
        _, _, n_slots, n_sems = make_plan(sizes, H)
        columns = sizes["dp"] * sizes["lat"] * sizes["lon"] * R * L
        factor = 1.0 / math.sqrt(columns)
        N = R * L
        any_spec = pl.BlockSpec(memory_space=pl.ANY)
        vmem_spec = pl.BlockSpec(memory_space=pltpu.VMEM)
        tile = pltpu.VMEM((R, C, L), F32)
        scratch = [
            pltpu.VMEM((C, R, L), F32), pltpu.VMEM((C, R, L), F32),
            pltpu.VMEM((H, C), BF16), pltpu.VMEM((C, H), BF16),
            pltpu.VMEM((C, H), BF16), pltpu.VMEM((H, C), BF16),
            pltpu.VMEM((H, L), F32),
            tile, tile, tile, tile, tile, tile,
            pltpu.VMEM((C, N), BF16), pltpu.VMEM((C, N), BF16), pltpu.VMEM((C, N), BF16),
            pltpu.VMEM((2, R, 1, L), F32),
            pltpu.VMEM((H, N), BF16), pltpu.VMEM((H, N), BF16),
            pltpu.VMEM((H, N), F32), pltpu.VMEM((H, N), F32), pltpu.VMEM((H, N), BF16),
            pltpu.VMEM((2 * H, C), F32), pltpu.VMEM((2 * H, C), F32), pltpu.VMEM((n_slots, C), F32),
            pltpu.VMEM((4, 2 * R, C), F32), pltpu.VMEM((4, 2, C, L), F32), pltpu.VMEM((4, L, C), F32),
            pltpu.VMEM((C, R, L), F32), pltpu.VMEM((C, R, L), F32),
            pltpu.SemaphoreType.DMA((4,)), pltpu.SemaphoreType.DMA((3 + H // L,)),
            pltpu.SemaphoreType.DMA((4, 2)), pltpu.SemaphoreType.DMA((4, 2)),
            pltpu.SemaphoreType.DMA((4, 2)), pltpu.SemaphoreType.DMA((4, 2)),
            pltpu.SemaphoreType.DMA((n_sems,)), pltpu.SemaphoreType.DMA((n_sems,)),
        ]
        return pl.pallas_call(
            functools.partial(kernel, sizes, factor),
            out_shape=(
                jax.ShapeDtypeStruct(initial_state.shape, F32), jax.ShapeDtypeStruct(initial_state.shape, F32),
                jax.ShapeDtypeStruct((H, C), F32), jax.ShapeDtypeStruct((C, H), F32),
            ),
            in_specs=[any_spec, any_spec, vmem_spec, vmem_spec, any_spec, vmem_spec, any_spec],
            out_specs=(any_spec,) * 4,
            scratch_shapes=scratch,
            compiler_params=pltpu.CompilerParams(
                collective_id=0, has_side_effects=True, vmem_limit_bytes=50 * 1024 * 1024),
            cost_estimate=pl.CostEstimate(flops=24 * H * C * N, bytes_accessed=4 * 1024 * 1024, transcendentals=2 * H * N),
        )(
            initial_state, cotangent, diffusion.reshape(1, C), norm_gain.reshape(1, C),
            weight_in, bias_in.reshape(H // L, L), weight_out,
        )

    return jax.shard_map(
        on_device, mesh=mesh, in_specs=(state, state, P(), P(), P(), P(), P()),
        out_specs=(state, state, P(), P()), check_vma=False,
    )
```

time: 246 us -> 62.5 us (0.25)
  waiting for transfers between devices: 155 us -> 0 us
  Pallas kernels: 0 us -> 53.7 us
  starting transfers between devices: 31.2 us -> 0 us
  matrix products: 15.2 us -> 0 us
  between operations: 14.4 us -> 0.67 us
  other arithmetic: 13.5 us -> 0 us
  local copies, waits for them, and re-layouts: 14.8 us -> 7.82 us
    psum x1 -> x0, waiting for transfers between devices: 106 us -> none  [on_device(): sum_in, sum_out = lax.psum((sum_in, sum_out), ('dp', 'lat', 'lon'))]
    pallas_call x0 -> x1, Pallas kernels: none -> 53.7 us  [on_device(): pl.pallas_call(functools.partial(kernel, sizes, factor), out_shape=(jax.S...]
    ppermute x16 -> x0, waiting for transfers between devices: 48.7 us -> none  [the longest x8 48.6 us: with_halo(): lax.ppermute(lax.slice_in_dim(block, 0, width, axis=dim), axis, backward)]
    ppermute x16 -> x0, starting transfers between devices: 31.2 us -> none  [the longest x8 20.4 us: with_halo(): lax.ppermute(lax.slice_in_dim(block, block.shape[dim] - width, None, axis...]
    dot_general x12 -> x0, matrix products: 15.2 us -> none  [the longest x2 4.21 us: on_device(): lax.dot_general(weight_out, adjoint_flat, CONTRACT_FIRST, preferred_eleme...]
    reduce_sum x4 -> x0, other arithmetic: 4.76 us -> none  [the longest x2 3.27 us: physics(): inverse = lax.rsqrt(jnp.mean(mixed * mixed, axis=0) + EPSILON)]
    slice x8 -> x0, local copies, waits for them, and re-layouts: 3.61 us -> none  [with_halo(): lax.slice_in_dim(block, 0, width, axis=dim)]
    reshape x4 -> x0, local copies, waits for them, and re-layouts: 3.49 us -> none  [the longest x2 2.27 us: on_device(): scaled_adj = normed_adj.reshape(mixed.shape) * norm_gain[:, None, None]]
  transfers between devices with their start and end apart: 17 -> 0, of which waited for: 5 -> 0; matrix products, arithmetic and copies ran while one was open for 2% -> 0% of each run, Pallas kernels for 0% -> 0%
where the time goes in v1:
time: 62.5 us; the launch traced here: 62.2 us
  Pallas kernels  53.7 us (86%)
  local copies, waits for them, and re-layouts  7.82 us (13%)
  between operations  0.67 us (1%)
    pallas_call x1, Pallas kernels, on_device(): pl.pallas_call(functools.partial(kernel, sizes, factor), out_shape=(jax.S...  53.7 us
    unnamed x18, local copies, waits for them, and re-layouts  7.82 us

profile of v1, /device:TPU:1, one launch (start us, length us, event | category | flops | bytes accessed | tf_op | source)
XLA Modules:
  0.0 62.2 jit_solution(6515758177579745563)
XLA Ops:
  0.6 0.0 copy-start.4
  0.6 0.0 copy-start.5
  0.7 0.0 copy-start.6
  0.7 0.7 %copy-done.4 = f32[1024]{0:T(1024)S(1)} copy-done((f32[1024]{0:T(1024)S(1)}, f32[1024]{0:T(1024)}, u32[]{:S(2)}) %copy-start.4) | copy-done | bytes 4120
  1.3 0.0 copy-done.5
  1.3 0.0 copy-done.6
  1.3 0.0 copy-start
  1.3 1.0 %copy-done = f32[1,128,8,128]{3,2,1,0:T(8,128)S(1)} copy-done((f32[1,128,8,128]{3,2,1,0:T(8,128)S(1)}, f32[1,128,8,128]{3,2,1,0:T(8,128)}, u32[]{:S(2)}) %copy-start) | copy-done | bytes 524312
  2.4 0.0 copy-start.1
  2.4 1.0 %copy-done.1 = f32[1,128,8,128]{3,2,1,0:T(8,128)S(1)} copy-done((f32[1,128,8,128]{3,2,1,0:T(8,128)S(1)}, f32[1,128,8,128]{3,2,1,0:T(8,128)}, u32[]{:S(2)}) %copy-start.1) | copy-done | bytes 524312
  3.4 0.0 copy-start.2
  3.4 0.9 %copy-done.2 = bf16[1024,128]{1,0:T(8,128)(2,1)S(1)} copy-done((bf16[1024,128]{1,0:T(8,128)(2,1)S(1)}, bf16[1024,128]{1,0:T(8,128)(2,1)}, u32[]{:S(2)}) %copy-start.2) | copy-done | bytes 262168
  4.4 0.0 copy-start.3
  4.4 0.9 %copy-done.3 = bf16[128,1024]{1,0:T(8,128)(2,1)S(1)} copy-done((bf16[128,1024]{1,0:T(8,128)(2,1)S(1)}, bf16[128,1024]{1,0:T(8,128)(2,1)}, u32[]{:S(2)}) %copy-start.3) | copy-done | bytes 262168
  5.3 53.7 %shard_map.102 = (f32[1,128,8,128]{3,2,1,0:T(8,128)S(1)}, f32[1,128,8,128]{3,2,1,0:T(8,128)S(1)}, f32[1024,128]{1,0:T(8,128)S(1)}, f32[128,1024]{1,0:T(8,128)S(1)}) custom-call(f32[1,128,8,128]{3,2,1,0:T(8,128)S(1)} %copy-done, f32[1,128,8,128]{3,2,1,0:T(8,128)S(1)} %copy-done.1, f32[1,128]{1,0:T(1,128)S(1)} %bitcast.4, f32[1,128]{1,0:T(1,128)S(1)} %bitcast.5, ...), custom_call_target="tpu_custom_call" | custom-call | flops 3221225472 | bytes 4194304 | tf_op jit(solution)/shard_map/pallas_call | solution.py:493
  59.0 0.8 %copy.15 = f32[1,128,8,128]{3,2,1,0:T(8,128)} copy(f32[1,128,8,128]{3,2,1,0:T(8,128)S(1)} %get-tuple-element.8) | data formatting | bytes 1048576
  59.8 0.8 %copy.16 = f32[1,128,8,128]{3,2,1,0:T(8,128)} copy(f32[1,128,8,128]{3,2,1,0:T(8,128)S(1)} %get-tuple-element.9) | data formatting | bytes 1048576
  60.6 0.8 %copy.17 = f32[1024,128]{1,0:T(8,128)} copy(f32[1024,128]{1,0:T(8,128)S(1)} %get-tuple-element.10) | data formatting | bytes 1048576
  61.4 0.8 %copy.18 = f32[128,1024]{1,0:T(8,128)} copy(f32[128,1024]{1,0:T(8,128)S(1)} %get-tuple-element.11) | data formatting | bytes 1048576
Async XLA Ops:
  0.6 0.7 %copy-start.4 = (f32[1024]{0:T(1024)S(1)}, f32[1024]{0:T(1024)}, u32[]{:S(2)}) copy-start(f32[1024]{0:T(1024)} %param.12) | copy-start | bytes 12292
  0.6 0.7 %copy-start.5 = (f32[128]{0:T(128)S(1)}, f32[128]{0:T(128)}, u32[]{:S(2)}) copy-start(f32[128]{0:T(128)} %param.9) | copy-start | bytes 1540
  0.7 0.7 %copy-start.6 = (f32[128]{0:T(128)S(1)}, f32[128]{0:T(128)}, u32[]{:S(2)}) copy-start(f32[128]{0:T(128)} %param.10) | copy-start | bytes 1540
  1.3 1.0 %copy-start = (f32[1,128,8,128]{3,2,1,0:T(8,128)S(1)}, f32[1,128,8,128]{3,2,1,0:T(8,128)}, u32[]{:S(2)}) copy-start(f32[1,128,8,128]{3,2,1,0:T(8,128)} %x_hbm.1) | copy-start | bytes 1572868
  2.4 1.0 %copy-start.1 = (f32[1,128,8,128]{3,2,1,0:T(8,128)S(1)}, f32[1,128,8,128]{3,2,1,0:T(8,128)}, u32[]{:S(2)}) copy-start(f32[1,128,8,128]{3,2,1,0:T(8,128)} %cot_hbm.1) | copy-start | bytes 1572868
  3.4 0.9 %copy-start.2 = (bf16[1024,128]{1,0:T(8,128)(2,1)S(1)}, bf16[1024,128]{1,0:T(8,128)(2,1)}, u32[]{:S(2)}) copy-start(bf16[1024,128]{1,0:T(8,128)(2,1)} %win_hbm.1) | copy-start | bytes 786436
  4.4 0.9 %copy-start.3 = (bf16[128,1024]{1,0:T(8,128)(2,1)S(1)}, bf16[128,1024]{1,0:T(8,128)(2,1)}, u32[]{:S(2)}) copy-start(bf16[128,1024]{1,0:T(8,128)(2,1)} %wout_hbm.1) | copy-start | bytes 786436

commit v2 on v1

--- a/solution.py
+++ b/solution.py
@@ -13,12 +13,14 @@
 F32 = jnp.float32
 BF16 = jnp.bfloat16
 NT = (((1,), (1,)), ((), ()))
+PARTS = 2
+UNROLL = True
 
 
 def make_plan(sizes, hidden):
     pair = 2 if sizes["lon"] % 2 == 0 else 1
-    counts = {"core": pair, "high": sizes["lon"] // pair, "lat": sizes["lat"], "dp": sizes["dp"]}
-    orders = (("core", "high", "lat", "dp"), ("core", "lat", "high", "dp"))
+    counts = {"core": pair, "plane": sizes["lon"] // pair * sizes["lat"], "dp": sizes["dp"]}
+    orders = (("core", "plane", "dp"),) * PARTS
     plan, slot, sem = [], 0, 0
     for stream in range(2):
         for part, order in enumerate(orders):
@@ -47,11 +49,11 @@
 def kernel(
     sizes, factor,
     x_hbm, cot_hbm, dif, gain, win_hbm, bias, wout_hbm,
-    fin_hbm, sg_hbm, gin_hbm, gout_hbm,
+    fin_v, sg_v, gin, gout,
     xin, cot, win, wout, winT, woutT, biasb,
     F0, F1, M0, M1, ADJ, MA, ADJB, NB0, NB1, INV, HID0, HID1, D0, HA, PA,
-    acc, res, slots, packed, halo_lat, halo_lon, fin_v, sg_v,
-    load_sem, store_sem, lat_send, lat_recv, lon_send, lon_recv, red_send, red_recv,
+    acc, res, slots, packed, halo_lat, halo_lon,
+    load_sem, lat_send, lat_recv, lon_send, lon_recv, red_send, red_recv,
 ):
     C, R, L = xin.shape
     H = win.shape[0]
@@ -71,11 +73,15 @@
         copy.start()
 
     barrier = pltpu.get_barrier_semaphore()
-    total = 0
-    for name, n, i in (("lon", n_lon, lon), ("lat", n_lat, lat), ("dp", n_dp, dp)):
-        for k in range(1, n):
-            pl.semaphore_signal(barrier, inc=1, device_id={name: lax.rem(i + k, n)}, device_id_type=MESH)
-            total += 1
+    greet = [{"lon": lax.rem(lon + 1, n_lon)}, {"lon": lax.rem(lon + n_lon - 1, n_lon)}]
+    plane, n_plane = lat * n_high + high, n_lat * n_high
+    for k in range(1, n_plane):
+        p = lax.rem(plane + k, n_plane)
+        greet.append({"lat": p // n_high, "lon": lax.rem(p, n_high) * pair + core})
+    for k in range(1, n_dp):
+        greet.append({"dp": lax.rem(dp + k, n_dp)})
+    for device in greet:
+        pl.semaphore_signal(barrier, inc=1, device_id=device, device_id_type=MESH)
 
     lane = lax.broadcasted_iota(jnp.int32, (C, L), 1)
 
@@ -123,8 +129,7 @@
         def _():
             up().start()
 
-    def send_lon(e, src):
-        pack(e, src)
+    def send_lon(e):
         for copy in lon_copies(e):
             copy.start()
 
@@ -186,13 +191,15 @@
     def span(q, width):
         return pl.ds(pl.multiple_of(q * width, width), width)
 
+    def loop(lo, hi, body):
+        lax.fori_loop(lo, hi, body, 0, unroll=UNROLL)
+
     def line(axis, i_n):
         if axis == "core":
             return core, lambda p: {"lon": high * pair + p}
-        if axis == "high":
-            return high, lambda p: {"lon": p * pair + core}
-        if axis == "lat":
-            return lat, lambda p: {"lat": p}
+        if axis == "plane":
+            return lat * n_high + high, lambda p: {
+                "lat": p // n_high, "lon": lax.rem(p, n_high) * pair + core}
         return dp, lambda p: {"dp": p}
 
     sent = []
@@ -265,27 +272,36 @@
             going = next(g, "end") is None or going
         return going
 
+    for e in range(4):
+        halo_lon[e, 2 * R:, :] = jnp.zeros((L - 2 * R, C), F32)
+    gT = jnp.broadcast_to(gain[...], (L, C)).T
+    for b in range(H // L):
+        biasb[b * L:(b + 1) * L, :] = jnp.broadcast_to(bias[b:b + 1, :], (L, L)).T
     loads[0].wait()
     for r in range(R):
         F0[r] = xin[:, r, :]
-    for e in range(4):
-        halo_lon[e, 2 * R:, :] = jnp.zeros((L - 2 * R, C), F32)
-    if total:
-        pl.semaphore_wait(barrier, total)
-    send_lat(0, F0)
-    send_lon(0, F0)
-    gT = jnp.broadcast_to(gain[...], (L, C)).T
-    for b in range(H // L):
-        biasb[b * L:(b + 1) * L, :] = jnp.broadcast_to(bias[b:b + 1, :], (L, L)).T
+    pack(0, F0)
     loads[1].wait()
     loads[2].wait()
     winT[...] = win[...].T
     woutT[...] = wout[...].T
+    pl.semaphore_wait(barrier, len(greet))
+    send_lat(0, F0)
+    send_lon(0)
     loads[3].wait()
     for r in range(R):
         a = cot[:, r, :]
         ADJ[r] = a
         ADJB[:, r * L:(r + 1) * L] = a.astype(BF16)
+
+    def early_adjoint(q, carry):
+        cols = span(q, W)
+        aq = ADJB[:, cols]
+        for h in range(0, H, HB):
+            HA[h:h + HB, cols] = jnp.dot(woutT[h:h + HB, :], aq, preferred_element_type=F32)
+        return carry
+
+    loop(0, R // 4, early_adjoint)
     wait_halo(0, F0)
 
     def put_m0(r, m):
@@ -309,18 +325,12 @@
         F1[2 * q + 1] = M0[2 * q + 1] + update[:, L:]
         return carry
 
-    lax.fori_loop(0, R // 2, forward0, 0)
+    loop(0, R // 2, forward0)
     send_lat(1, F1)
-    send_lon(1, F1)
-
-    def early_adjoint(q, carry):
-        cols = span(q, W)
-        aq = ADJB[:, cols]
-        for h in range(0, H, HB):
-            HA[h:h + HB, cols] = jnp.dot(woutT[h:h + HB, :], aq, preferred_element_type=F32)
-        return carry
-
-    lax.fori_loop(0, R // 2, early_adjoint, 0)
+    pack(1, F1)
+    send_lon(1)
+
+    loop(R // 4, R // 2, early_adjoint)
     wait_halo(1, F1)
 
     def put_m1(r, m):
@@ -357,9 +367,10 @@
         return carry
 
     wait_sent(0, F0)
-    lax.fori_loop(0, R // 2, forward1, 0)
+    loop(0, R // 2, forward1)
     send_lat(2, MA)
-    send_lon(2, MA)
+    pack(2, MA)
+    send_lon(2)
 
     def terms_out(hid_ref, add):
         def body(j, carry):
@@ -370,7 +381,7 @@
                 part = t[:, k * L:(k + 1) * L]
                 acc[at, :] = acc[at, :] + part if add else part
             return carry
-        lax.fori_loop(0, H // HB, body, 0)
+        loop(0, H // HB, body)
 
     def terms_in(nb, add, lo, hi):
         def body(j, carry):
@@ -378,14 +389,12 @@
             t = lax.dot_general(PA[rows, :], nb[...], NT, preferred_element_type=F32)
             acc[rows, :] = acc[rows, :] + t if add else t
             return carry
-        lax.fori_loop(lo, hi, body, 0)
+        loop(lo, hi, body)
 
     terms_out(HID1, False)
     terms_in(NB1, False, 0, H // HB)
     for r in range(R):
-        fin_v[:, r, :] = F0[r]
-    fin_store = pltpu.make_async_copy(fin_v, fin_hbm.at[0], store_sem.at[0])
-    fin_store.start()
+        fin_v[0, :, r, :] = F0[r]
     wait_halo(2, MA)
 
     def put_adj(r, a):
@@ -404,7 +413,7 @@
             PA[h:h + HB, cols] = (ha * D0[h:h + HB, cols]).astype(BF16)
         return carry
 
-    lax.fori_loop(0, R // 2, back0, 0)
+    loop(0, R // 2, back0)
     advance(out_streams)
     blocks = H // HB
     for s, g in enumerate(in_streams):
@@ -420,42 +429,27 @@
             mix(0, 2 * q + k, M0, na[:, k * L:(k + 1) * L], gt)
         return carry
 
-    lax.fori_loop(0, R // 2, back1, 0)
+    loop(0, R // 2, back1)
     send_lat(3, MA)
-    send_lon(3, MA)
+    pack(3, MA)
+    send_lon(3)
     advance(out_streams)
     advance(in_streams)
     wait_halo(3, MA)
 
     def put_grad(r, a):
-        sg_v[:, r, :] = a
+        sg_v[0, :, r, :] = a
 
     diffuse(3, MA, put_grad)
-    sg_store = pltpu.make_async_copy(sg_v, sg_hbm.at[0], store_sem.at[1])
-    sg_store.start()
-    stores = [fin_store, sg_store]
-    out_going = in_going = True
-    while out_going or in_going:
-        if out_going:
-            out_going = advance(out_streams)
-            if not out_going:
-                for b in range(H // L):
-                    copy = pltpu.make_async_copy(
-                        res.at[pl.ds(H + b * L, C)], gout_hbm.at[:, pl.ds(b * L, L)], store_sem.at[3 + b])
-                    copy.start()
-                    stores.append(copy)
-        if in_going:
-            in_going = advance(in_streams)
-            if not in_going:
-                copy = pltpu.make_async_copy(res.at[pl.ds(0, H)], gin_hbm, store_sem.at[2])
-                copy.start()
-                stores.append(copy)
+    while advance(out_streams + in_streams):
+        pass
+    gin[...] = res[0:H]
+    for b in range(H // L):
+        gout[:, b * L:(b + 1) * L] = res[H + b * L:H + b * L + C]
     for copy in sent:
         copy.wait_send()
     wait_sent(1, F1)
     wait_sent(3, MA)
-    for copy in stores:
-        copy.wait()
 
 
 def solution(mesh):
@@ -469,7 +463,6 @@
         columns = sizes["dp"] * sizes["lat"] * sizes["lon"] * R * L
         factor = 1.0 / math.sqrt(columns)
         N = R * L
-        any_spec = pl.BlockSpec(memory_space=pl.ANY)
         vmem_spec = pl.BlockSpec(memory_space=pltpu.VMEM)
         tile = pltpu.VMEM((R, C, L), F32)
         scratch = [
@@ -484,23 +477,21 @@
             pltpu.VMEM((H, N), F32), pltpu.VMEM((H, N), F32), pltpu.VMEM((H, N), BF16),
             pltpu.VMEM((2 * H, C), F32), pltpu.VMEM((2 * H, C), F32), pltpu.VMEM((n_slots, C), F32),
             pltpu.VMEM((4, 2 * R, C), F32), pltpu.VMEM((4, 2, C, L), F32), pltpu.VMEM((4, L, C), F32),
-            pltpu.VMEM((C, R, L), F32), pltpu.VMEM((C, R, L), F32),
-            pltpu.SemaphoreType.DMA((4,)), pltpu.SemaphoreType.DMA((3 + H // L,)),
+            pltpu.SemaphoreType.DMA((4,)),
             pltpu.SemaphoreType.DMA((4, 2)), pltpu.SemaphoreType.DMA((4, 2)),
             pltpu.SemaphoreType.DMA((4, 2)), pltpu.SemaphoreType.DMA((4, 2)),
             pltpu.SemaphoreType.DMA((n_sems,)), pltpu.SemaphoreType.DMA((n_sems,)),
         ]
+        shape = jax.ShapeDtypeStruct(initial_state.shape, F32)
+        hbm_spec = pl.BlockSpec(memory_space=pltpu.HBM)
         return pl.pallas_call(
             functools.partial(kernel, sizes, factor),
-            out_shape=(
-                jax.ShapeDtypeStruct(initial_state.shape, F32), jax.ShapeDtypeStruct(initial_state.shape, F32),
-                jax.ShapeDtypeStruct((H, C), F32), jax.ShapeDtypeStruct((C, H), F32),
-            ),
-            in_specs=[any_spec, any_spec, vmem_spec, vmem_spec, any_spec, vmem_spec, any_spec],
-            out_specs=(any_spec,) * 4,
+            out_shape=(shape, shape, jax.ShapeDtypeStruct((H, C), F32), jax.ShapeDtypeStruct((C, H), F32)),
+            in_specs=[hbm_spec, hbm_spec, vmem_spec, vmem_spec, hbm_spec, vmem_spec, hbm_spec],
+            out_specs=(vmem_spec,) * 4,
             scratch_shapes=scratch,
             compiler_params=pltpu.CompilerParams(
-                collective_id=0, has_side_effects=True, vmem_limit_bytes=50 * 1024 * 1024),
+                collective_id=0, has_side_effects=True, vmem_limit_bytes=60 * 1024 * 1024),
             cost_estimate=pl.CostEstimate(flops=24 * H * C * N, bytes_accessed=4 * 1024 * 1024, transcendentals=2 * H * N),
         )(
             initial_state, cotangent, diffusion.reshape(1, C), norm_gain.reshape(1, C),

time: 62.5 us -> 55.4 us (0.89)
  Pallas kernels: 53.7 us -> 49.2 us
  local copies, waits for them, and re-layouts: 7.82 us -> 5.18 us
    pallas_call x1, Pallas kernels: 53.7 us -> 49.2 us  [on_device(): pl.pallas_call(functools.partial(kernel, sizes, factor), out_shape=(shape...]
    unnamed x18 -> x10, local copies, waits for them, and re-layouts: 7.82 us -> 5.18 us
where the time goes in v2:
time: 55.4 us; the launch traced here: 55.1 us
  Pallas kernels  49.2 us (89%)
  local copies, waits for them, and re-layouts  5.18 us (9%)
  between operations  0.65 us (1%)
    pallas_call x1, Pallas kernels, on_device(): pl.pallas_call(functools.partial(kernel, sizes, factor), out_shape=(shape...  49.2 us
    unnamed x10, local copies, waits for them, and re-layouts  5.18 us

profile of v2, /device:TPU:1, one launch (start us, length us, event | category | flops | bytes accessed | tf_op | source)
XLA Modules:
  0.0 55.1 jit_solution(11153560713914701719)
XLA Ops:
  0.6 49.2 %shard_map.102 = (f32[1,128,8,128]{3,2,1,0:T(8,128)}, f32[1,128,8,128]{3,2,1,0:T(8,128)}, f32[1024,128]{1,0:T(8,128)}, f32[128,1024]{1,0:T(8,128)}) custom-call(f32[1,128,8,128]{3,2,1,0:T(8,128)} %x_hbm.1, f32[1,128,8,128]{3,2,1,0:T(8,128)} %cot_hbm.1, f32[1,128]{1,0:T(1,128)} %bitcast.4, f32[1,128]{1,0:T(1,128)} %bitcast.5, bf16[1024,128]{1,0:T(8,128)(2,1)} %win_hbm.1, ...), custom_call_target="tpu_custom_call" | custom-call | flops 3221225472 | bytes 4194304 | tf_op jit(solution)/shard_map/pallas_call | solution.py:487
  49.9 0.0 copy-start.2
  49.9 1.9 %copy.15 = f32[1,128,8,128]{3,2,1,0:T(8,128)} copy(f32[1,128,8,128]{3,2,1,0:T(8,128)} %get-tuple-element.8) | data formatting | bytes 1048576
  51.8 0.0 copy-done.2
  51.8 0.0 copy-start.1
  51.8 0.8 %copy.16 = f32[1,128,8,128]{3,2,1,0:T(8,128)} copy(f32[1,128,8,128]{3,2,1,0:T(8,128)S(1)} %copy-done.2) | data formatting | bytes 1048576
  52.6 0.4 copy-done.1
  53.0 0.0 copy-start
  53.0 0.8 %copy.17 = f32[1024,128]{1,0:T(8,128)} copy(f32[1024,128]{1,0:T(8,128)S(1)} %copy-done.1) | data formatting | bytes 1048576
  53.8 0.4 copy-done
  54.3 0.8 %copy.18 = f32[128,1024]{1,0:T(8,128)} copy(f32[128,1024]{1,0:T(8,128)S(1)} %copy-done) | data formatting | bytes 1048576
Async XLA Ops:
  49.9 1.9 %copy-start.2 = (f32[1,128,8,128]{3,2,1,0:T(8,128)S(1)}, f32[1,128,8,128]{3,2,1,0:T(8,128)}, u32[]{:S(2)}) copy-start(f32[1,128,8,128]{3,2,1,0:T(8,128)} %get-tuple-element.9) | copy-start | bytes 1572868
  51.8 1.2 %copy-start.1 = (f32[1024,128]{1,0:T(8,128)S(1)}, f32[1024,128]{1,0:T(8,128)}, u32[]{:S(2)}) copy-start(f32[1024,128]{1,0:T(8,128)} %get-tuple-element.10) | copy-start | bytes 1572868
  53.0 1.2 %copy-start = (f32[128,1024]{1,0:T(8,128)S(1)}, f32[128,1024]{1,0:T(8,128)}, u32[]{:S(2)}) copy-start(f32[128,1024]{1,0:T(8,128)} %get-tuple-element.11) | copy-start | bytes 1572868
